TPU v7x, 1024 devices: a whole 8x8x8 slice. The times are simulated.
1024 devices in a mesh: fsdp: 64 (over z, y), rep: 16 (over x, core).
Axes of the slice: x: 8, y: 8, z: 8, core: 2. Of those that a mesh axis runs over, the one named last changes fastest.
Arguments:
- grad_parts: bfloat16 [16, 4096, 16, 256], P('rep', 'fsdp'), may hold values from -0.3125 to 0.3125
- slot_block: int32 [64, 2], replicated, may hold values from -1 to 63, as said below
- stat_left: float32 [64, 2, 1024, 1024], P('fsdp', None, 'rep'), as said below
- stat_right: float32 [64, 2, 1024, 1024], P('fsdp', None, 'rep'), as said below
- root_left: bfloat16 [64, 2, 1024, 1024], P('fsdp'), as said below
- root_right: bfloat16 [64, 2, 1024, 1024], P('fsdp', None, None, 'rep'), as said below
Outputs:
- new_left: float32 [64, 2, 1024, 1024], P('fsdp', None, 'rep')
- new_right: float32 [64, 2, 1024, 1024], P('fsdp', None, 'rep')
- precond: bfloat16 [4096, 16, 1024], P('fsdp', None, 'rep')
Inputs may be any that keep to these rules, and one draw needn't show every extreme that they name: `slot_block`: every block number 0 to 63 stands in exactly one slot; all other slots hold -1; no owner holds more than 1 block of one band (blocks a * 16 to (a + 1) * 16 - 1), and some owner holds exactly 1 of some band; in every draw some owner has all 2 slots filled, and loads differ between owners. `stat_left`: Symmetric. `stat_right`: Symmetric. `root_left`: Symmetric. `root_right`: Symmetric.
All inputs are finite; a program needn't handle non-finite values.
Results may differ from a plain program's by a relative error of at most 0.015.
Values may be sent and summed in bfloat16 or wider, within the bound.
No kernel may reach another device: no remote copies, remote signals or barrier semaphores. Data moves between devices by JAX's collectives and lax.ppermute only.
A program may use at most 64 MiB of HBM per device.

v0:
```python
import jax
import jax.numpy as jnp
from jax import lax
from jax.experimental import pallas as pl
from jax.experimental.pallas import tpu as pltpu
from jax.sharding import PartitionSpec as P

STAT_DECAY = 0.9


def over_core(value):
    size = lax.axis_size("rep")
    both = lax.all_gather(
        value, "rep", axis_index_groups=[[r, r + 1] for r in range(0, size, 2)]
    )
    return taken(both, 1 - lax.axis_index("rep") % 2)


def exchanged(value, mask):
    size = lax.axis_size("rep")
    return lax.ppermute(value, "rep", [(r, r ^ mask) for r in range(size)])


def passed(value, step):
    size = lax.axis_size("rep")
    return lax.ppermute(value, "rep", [(r, (r + step) % size) for r in range(size)])


def taken(value, index):
    return lax.dynamic_index_in_dim(value, index, 0, keepdims=False)


def either(first, own, other):
    return jnp.where(first, own, other), jnp.where(first, other, own)


def finish_kernel(
    core_ref, far_place_ref, own_place_ref,
    near_ref, far_ref, right_ref, left_ref, blank_ref,
    own_ref, given_ref, middle_ref,
):
    f32 = jnp.float32

    @pl.when(pl.program_id(0) == 0)
    def _():
        last = jnp.dot(far_ref[...], right_ref[0], preferred_element_type=f32)
        middle_ref[...] = (near_ref[...] + last).astype(middle_ref.dtype)

    result = jnp.dot(left_ref[0, 0], middle_ref[...], preferred_element_type=f32)
    sources, half, wide = given_ref.shape
    slab = wide // 2
    low = lax.broadcasted_iota(jnp.int32, (half, wide), 1) < slab
    for i in range(sources):
        upper = result[2 * i * half : (2 * i + 1) * half]
        lower = result[(2 * i + 1) * half : (2 * i + 2) * half]
        zero = jnp.where(low, upper, pltpu.roll(lower, slab, 1)).astype(given_ref.dtype)
        one = jnp.where(low, pltpu.roll(upper, slab, 1), lower).astype(given_ref.dtype)

        @pl.when(core_ref[0] == 0)
        def _():
            own_ref[0, i] = zero
            given_ref[i] = one

        @pl.when(core_ref[0] != 0)
        def _():
            own_ref[0, i] = one
            given_ref[i] = zero


def finish(core, far_place, own_place, near, far, right, left, blank):
    block, wide = far.shape
    _, sources, half, _ = blank.shape
    steps = 4
    few = sources // steps
    return pl.pallas_call(
        finish_kernel,
        grid_spec=pltpu.PrefetchScalarGridSpec(
            num_scalar_prefetch=3,
            grid=(steps,),
            in_specs=[
                pl.BlockSpec((block, wide), lambda i, c, f, o: (0, 0)),
                pl.BlockSpec((block, wide), lambda i, c, f, o: (0, 0)),
                pl.BlockSpec((1, wide, wide), lambda i, c, f, o: (f[0], 0, 0)),
                pl.BlockSpec((1, 1, block // steps, block), lambda i, c, f, o: (0, c[0], i, 0)),
                pl.BlockSpec(memory_space=pl.ANY),
            ],
            out_specs=[
                pl.BlockSpec((1, few, half, wide), lambda i, c, f, o: (o[0], i, 0, 0)),
                pl.BlockSpec((few, half, wide), lambda i, c, f, o: (i, 0, 0)),
            ],
            scratch_shapes=[pltpu.VMEM((block, wide), far.dtype)],
        ),
        out_shape=[
            jax.ShapeDtypeStruct(blank.shape, blank.dtype),
            jax.ShapeDtypeStruct((sources, half, wide), far.dtype),
        ],
        input_output_aliases={7: 0},
        compiler_params=pltpu.CompilerParams(vmem_limit_bytes=24 * 2**20),
    )(core.reshape(1), far_place.reshape(1), own_place.reshape(1), near, far, right, left, blank)


def local(grad_parts, slot_block, stat_left, stat_right, root_left, root_right):
    bf16, f32 = jnp.bfloat16, jnp.float32
    shard_rows, col_blocks = grad_parts.shape[1:3]
    block = stat_left.shape[3]
    owners, slot_count = slot_block.shape
    slab = root_right.shape[3]
    wide = 2 * slab
    chips = block // wide
    sources = block // shard_rows
    bands = owners // sources
    half = shard_rows // 2
    shard = lax.axis_index("fsdp")
    member = lax.axis_index("rep")
    core, chip = member % 2, member // 2
    first = core == 0
    my_band = shard // sources

    block_column = slot_block - my_band * col_blocks
    in_band = (slot_block >= 0) & (block_column >= 0) & (block_column < col_blocks)
    sends = jnp.any(
        in_band[:, :, None] & (block_column[:, :, None] == jnp.arange(col_blocks)), axis=1
    )
    owner_of = jnp.argmax(sends, axis=0)
    held = taken(slot_block, shard)
    held_band = held // col_blocks
    spare_band = (jnp.max(held_band) + 1) % bands
    places = jnp.where(held >= 0, held_band, spare_band).astype(jnp.uint32)
    own_place, other_place = either(first, places[0], places[1])

    partial = grad_parts[0]
    kept = lax.dynamic_slice_in_dim(partial, core * half, half, 0)
    given = lax.dynamic_slice_in_dim(partial, (1 - core) * half, half, 0)
    pair = kept.astype(f32) + over_core(given).astype(f32)
    side = chip % 2
    kept = lax.dynamic_slice_in_dim(pair, side * wide, wide, 2)
    given = lax.dynamic_slice_in_dim(pair, (1 - side) * wide, wide, 2)
    gradient = (kept + exchanged(given.astype(bf16), 2).astype(f32)).astype(bf16)

    outgoing = jnp.einsum(
        "oc,rcj->orj", sends.astype(bf16), gradient, preferred_element_type=f32
    ).astype(bf16)
    arrived = lax.all_to_all(outgoing, "fsdp", split_axis=0, concat_axis=0, tiled=True)
    blank = jnp.full((owners, half, wide), own_place // jnp.uint32(bands), bf16)
    arrived, own_place, other_place = lax.optimization_barrier(
        (arrived, own_place, other_place)
    )
    banded = arrived.reshape(bands, sources, half, wide)
    own, other = taken(banded, own_place), taken(banded, other_place)

    upper, lower = either(first, own, over_core(other))
    piece = jnp.stack([upper, lower], axis=1).reshape(block, wide)
    right_pair = either(
        first, taken(root_right[0], core), over_core(taken(root_right[0], 1 - core))
    )
    right = jnp.concatenate(right_pair, axis=1).reshape(chips, wide, wide)

    up, down = [piece], [piece]
    for _ in range(chips // 2 - 1):
        up.append(passed(up[-1], 2))
        down.append(passed(down[-1], -2))
    far = passed(up[-1], 2)

    def part(away, columns):
        rows = taken(right, ((chip + away) % chips).astype(jnp.uint32))
        return jnp.dot(columns, rows, preferred_element_type=f32)

    near = part(0, piece)
    for away in range(1, chips // 2):
        near = near + (part(away, down[away]) + part(chips - away, up[away]))
        if away == 1:
            near, blank = lax.optimization_barrier((near, blank))

    blank = blank.reshape(bands, sources, half, wide)
    far_place = (chip + chips // 2) % chips
    returning, given = finish(
        core, far_place, own_place.astype(jnp.int32), near, far, right, root_left, blank
    )
    returning = lax.dynamic_update_index_in_dim(returning, over_core(given), other_place, 0)
    returning = returning.reshape(owners, half, wide)
    slabs = down + [far] + up[:0:-1]
    *slabs, returning = lax.optimization_barrier((*slabs, returning))
    came_back = lax.all_to_all(returning, "fsdp", split_axis=0, concat_axis=0, tiled=True)
    picked = jnp.take(came_back, owner_of, axis=0)
    precond = jnp.concatenate([picked[:, :, :slab], picked[:, :, slab:]], axis=1)
    precond = precond.transpose(1, 0, 2)

    piece = slabs[0]
    whole = jnp.concatenate(slabs, axis=1)
    rows = lax.dynamic_slice_in_dim(whole, chip * wide, wide, 0)
    left_rows = jnp.einsum("ic,kc->ik", rows, whole, preferred_element_type=f32)
    right_rows = jnp.einsum("ki,kc->ic", piece, whole, preferred_element_type=f32)
    right_rows = lax.dynamic_slice_in_dim(
        jnp.concatenate([right_rows, right_rows], axis=1),
        (chips - chip) % chips * wide,
        block,
        1,
    )
    both = jnp.stack([left_rows, right_rows])
    own = lax.dynamic_slice_in_dim(both, core * slab, slab, 1)
    other = exchanged(lax.dynamic_slice_in_dim(both, (1 - core) * slab, slab, 1), 1)
    products = jnp.stack(either(first, own, other), axis=1)
    new_left = STAT_DECAY * stat_left[0] + (1.0 - STAT_DECAY) * products[0]
    new_right = STAT_DECAY * stat_right[0] + (1.0 - STAT_DECAY) * products[1]
    return (new_left[None], new_right[None], precond)


def solution(mesh):
    placed = (
        P("rep", "fsdp", None, None),
        P(),
        P("fsdp", None, "rep", None),
        P("fsdp", None, "rep", None),
        P("fsdp", None, None, None),
        P("fsdp", None, None, "rep"),
    )
    return jax.shard_map(
        local,
        mesh=mesh,
        in_specs=placed,
        out_specs=(
            P("fsdp", None, "rep", None),
            P("fsdp", None, "rep", None),
            P("fsdp", None, "rep"),
        ),
        check_vma=False,
    )
```

profile of v0, /device:TPU:8, one launch (start us, length us, event | category | flops | bytes accessed | tf_op | source)
XLA Modules:
  0.0 132.1 jit_solution(169613851469340866)
XLA Ops:
  0.7 1.0 constant_dynamic-slice_fusion.3
  1.7 2.2 %all_gather.18 = bf16[2,32,16,256]{3,2,1,0:T(8,128)(2,1)S(1)} all-gather(bf16[1,32,16,256]{3,2,1,0:T(8,128)(2,1)S(1)} %constant_dynamic-slice_fusion.3), channel_id=1, replica_groups={{0,1},{2,3},{4,5},{6,7},{8,9},{10,11},{12,13},{14,15},{16,17},{18,19},{..., dimensions={0}, use_global_device_ids=true | all-gather | bytes 786432 | tf_op jit(solution)/shard_map/all_gather | solution.py:13
  3.9 1.1 convert_add_fusion
  5.0 2.5 %collective-permute-start = (bf16[32,16,128]{2,1,0:T(8,128)(2,1)S(1)}, bf16[32,16,128]{2,1,0:T(8,128)(2,1)S(1)}, u32[]{:S(2)}, u32[]{:S(2)}) collective-permute-start(bf16[32,16,128]{2,1,0:T(8,128)(2,1)S(1)} %fusion.16), channel_id=1, source_target_pairs={{0,2},{1,3},{2,0},{3,1},{4,6},{5,7},{6,4},{7,5},{8,10},{9,11},{10,... | collective-permute-start | bytes 393224 | tf_op jit(solution)/shard_map/ppermute | solution.py:21
  7.7 4.6 %collective-permute-done = bf16[32,16,128]{2,1,0:T(8,128)(2,1)S(1)} collective-permute-done((bf16[32,16,128]{2,1,0:T(8,128)(2,1)S(1)}, bf16[32,16,128]{2,1,0:T(8,128)(2,1)S(1)}, u32[]{:S(2)}, u32[]{:S(2)}) %collective-permute-start) | collective-permute-done | bytes 131104 | tf_op jit(solution)/shard_map/ppermute | solution.py:21
  12.7 1.1 copy.45
  13.9 23.4 %all-to-all-start = ((bf16[64,32,128]{2,1,0:T(8,128)(2,1)}), bf16[64,32,128]{2,1,0:T(8,128)(2,1)S(1)}, u32[]{:S(2)}, u32[]{:S(2)}) async-start(bf16[64,32,128]{2,1,0:T(8,128)(2,1)} %copy.45), calls=%async_computation | async-start | bytes 1048576 | tf_op jit(solution)/shard_map/all_to_all | solution.py:143
  41.9 2.0 %all-gather = bf16[2,1,1024,64]{2,3,1,0:T(8,128)(2,1)S(1)} all-gather(bf16[1,1,1024,64]{2,3,1,0:T(8,128)(2,1)S(1)} %constant_dynamic-slice_fusion.1), channel_id=2, replica_groups={{0,1},{2,3},{4,5},{6,7},{8,9},{10,11},{12,13},{14,15},{16,17},{18,19},{..., dimensions={0}, use_global_device_ids=true | all-gather | bytes 393216 | tf_op jit(solution)/shard_map/all_gather | solution.py:13
  44.9 11.4 %all-to-all-done = bf16[64,32,128]{2,1,0:T(8,128)(2,1)S(1)} async-done(((bf16[64,32,128]{2,1,0:T(8,128)(2,1)}), bf16[64,32,128]{2,1,0:T(8,128)(2,1)S(1)}, u32[]{:S(2)}, u32[]{:S(2)}) %all-to-all-start) | async-done | bytes 524320 | tf_op jit(solution)/shard_map/all_to_all | solution.py:143
  56.4 2.0 %all_gather.19 = bf16[2,16,32,128]{3,2,1,0:T(8,128)(2,1)S(1)} all-gather(bf16[1,16,32,128]{3,2,1,0:T(8,128)(2,1)S(1)} %constant_dynamic-slice_fusion), channel_id=1, replica_groups={{0,1},{2,3},{4,5},{6,7},{8,9},{10,11},{12,13},{14,15},{16,17},{18,19},{..., dimensions={0}, use_global_device_ids=true | all-gather | bytes 393216 | tf_op jit(solution)/shard_map/all_gather | solution.py:13
  58.5 2.5 %collective-permute-start.4 = (bf16[1024,128]{1,0:T(8,128)(2,1)S(1)}, bf16[1024,128]{1,0:T(8,128)(2,1)S(1)}, u32[]{:S(2)}, u32[]{:S(2)}) collective-permute-start(bf16[1024,128]{1,0:T(8,128)(2,1)S(1)} %bitcast.95), channel_id=1, source_target_pairs={{0,2},{1,3},{2,4},{3,5},{4,6},{5,7},{6,8},{7,9},{8,10},{9,11},{10,... | collective-permute-start | bytes 786440 | tf_op jit(solution)/shard_map/ppermute | solution.py:26
  61.0 4.6 %collective-permute-start.1 = (bf16[1024,128]{1,0:T(8,128)(2,1)S(1)}, bf16[1024,128]{1,0:T(8,128)(2,1)S(1)}, u32[]{:S(2)}, u32[]{:S(2)}) collective-permute-start(bf16[1024,128]{1,0:T(8,128)(2,1)S(1)} %bitcast.96), channel_id=1, source_target_pairs={{0,14},{1,15},{2,0},{3,1},{4,2},{5,3},{6,4},{7,5},{8,6},{9,7},{10,... | collective-permute-start | bytes 786440 | tf_op jit(solution)/shard_map/ppermute | solution.py:26
  66.2 3.7 %collective-permute-done.4 = bf16[1024,128]{1,0:T(8,128)(2,1)S(1)} collective-permute-done((bf16[1024,128]{1,0:T(8,128)(2,1)S(1)}, bf16[1024,128]{1,0:T(8,128)(2,1)S(1)}, u32[]{:S(2)}, u32[]{:S(2)}) %collective-permute-start.4) | collective-permute-done | bytes 262176 | tf_op jit(solution)/shard_map/ppermute | solution.py:26
  70.0 1.9 %collective-permute-start.5 = (bf16[1024,128]{1,0:T(8,128)(2,1)S(1)}, bf16[1024,128]{1,0:T(8,128)(2,1)S(1)}, u32[]{:S(2)}, u32[]{:S(2)}) collective-permute-start(bf16[1024,128]{1,0:T(8,128)(2,1)S(1)} %collective-permute-done.4), channel_id=1, source_target_pairs={{0,2},{1,3},{2,4},{3,5},{4,6},{5,7},{6,8},{7,9},{8,10},{9,11},{10,... | collective-permute-start | bytes 786440 | tf_op jit(solution)/shard_map/ppermute | solution.py:26
  71.9 5.1 %collective-permute-start.2 = (bf16[1024,128]{1,0:T(8,128)(2,1)S(1)}, bf16[1024,128]{1,0:T(8,128)(2,1)S(1)}, u32[]{:S(2)}, u32[]{:S(2)}) collective-permute-start(bf16[1024,128]{1,0:T(8,128)(2,1)S(1)} %collective-permute-done.1), channel_id=1, source_target_pairs={{0,14},{1,15},{2,0},{3,1},{4,2},{5,3},{6,4},{7,5},{8,6},{9,7},{10,... | collective-permute-start | bytes 786440 | tf_op jit(solution)/shard_map/ppermute | solution.py:26
  77.6 0.9 broadcast_in_dim.27
  78.5 2.1 %collective-permute-done.5 = bf16[1024,128]{1,0:T(8,128)(2,1)S(1)} collective-permute-done((bf16[1024,128]{1,0:T(8,128)(2,1)S(1)}, bf16[1024,128]{1,0:T(8,128)(2,1)S(1)}, u32[]{:S(2)}, u32[]{:S(2)}) %collective-permute-start.5) | collective-permute-done | bytes 262176 | tf_op jit(solution)/shard_map/ppermute | solution.py:26
  80.6 1.9 %collective-permute-start.6 = (bf16[1024,128]{1,0:T(8,128)(2,1)S(1)}, bf16[1024,128]{1,0:T(8,128)(2,1)S(1)}, u32[]{:S(2)}, u32[]{:S(2)}) collective-permute-start(bf16[1024,128]{1,0:T(8,128)(2,1)S(1)} %collective-permute-done.5), channel_id=1, source_target_pairs={{0,2},{1,3},{2,4},{3,5},{4,6},{5,7},{6,8},{7,9},{8,10},{9,11},{10,... | collective-permute-start | bytes 786440 | tf_op jit(solution)/shard_map/ppermute | solution.py:26
  82.5 5.1 %collective-permute-start.3 = (bf16[1024,128]{1,0:T(8,128)(2,1)S(1)}, bf16[1024,128]{1,0:T(8,128)(2,1)S(1)}, u32[]{:S(2)}, u32[]{:S(2)}) collective-permute-start(bf16[1024,128]{1,0:T(8,128)(2,1)S(1)} %collective-permute-done.2), channel_id=1, source_target_pairs={{0,14},{1,15},{2,0},{3,1},{4,2},{5,3},{6,4},{7,5},{8,6},{9,7},{10,... | collective-permute-start | bytes 786440 | tf_op jit(solution)/shard_map/ppermute | solution.py:26
  88.2 2.0 %collective-permute-done.6 = bf16[1024,128]{1,0:T(8,128)(2,1)S(1)} collective-permute-done((bf16[1024,128]{1,0:T(8,128)(2,1)S(1)}, bf16[1024,128]{1,0:T(8,128)(2,1)S(1)}, u32[]{:S(2)}, u32[]{:S(2)}) %collective-permute-start.6) | collective-permute-done | bytes 262176 | tf_op jit(solution)/shard_map/ppermute | solution.py:26
  90.3 1.9 %collective-permute-start.7 = (bf16[1024,128]{1,0:T(8,128)(2,1)S(1)}, bf16[1024,128]{1,0:T(8,128)(2,1)S(1)}, u32[]{:S(2)}, u32[]{:S(2)}) collective-permute-start(bf16[1024,128]{1,0:T(8,128)(2,1)S(1)} %collective-permute-done.6), channel_id=1, source_target_pairs={{0,2},{1,3},{2,4},{3,5},{4,6},{5,7},{6,8},{7,9},{8,10},{9,11},{10,... | collective-permute-start | bytes 786440 | tf_op jit(solution)/shard_map/ppermute | solution.py:26
  92.8 6.9 %collective-permute-done.7.far_ref = bf16[1024,128]{1,0:T(8,128)(2,1)S(1)} collective-permute-done((bf16[1024,128]{1,0:T(8,128)(2,1)S(1)}, bf16[1024,128]{1,0:T(8,128)(2,1)S(1)}, u32[]{:S(2)}, u32[]{:S(2)}) %collective-permute-start.7) | collective-permute-done | bytes 262176 | tf_op jit(solution)/shard_map/ppermute | solution.py:26
  99.7 3.0 %shard_map.85 = (bf16[4,16,32,128]{3,2,1,0:T(8,128)(2,1)}, bf16[16,32,128]{2,1,0:T(8,128)(2,1)S(1)}) custom-call(s32[1]{0:T(128)} %bitcast.10.core_ref, s32[1]{0:T(128)} %bitcast.11.far_place_ref, s32[1]{0:T(128)} %bitcast.12.own_place_ref, f32[1024,128]{1,0:T(8,128)S(1)} %fusion.2.near_ref, ...), custom_call_target="tpu_custom_call", output_to_operand_aliasing={{0}: (7, {})} | custom-call | tf_op jit(solution)/shard_map/pallas_call | solution.py:75
  102.8 2.0 %all-gather.1 = bf16[32,32,128]{2,1,0:T(8,128)(2,1)S(1)} all-gather(bf16[16,32,128]{2,1,0:T(8,128)(2,1)S(1)} %get-tuple-element.26), channel_id=3, replica_groups={{0,1},{2,3},{4,5},{6,7},{8,9},{10,11},{12,13},{14,15},{16,17},{18,19},{..., dimensions={0}, use_global_device_ids=true | all-gather | bytes 393216 | tf_op jit(solution)/shard_map/all_gather | solution.py:13
  104.8 0.7 dynamic-slice_dynamic-update-slice_fusion
  105.4 5.1 %all-to-all-start.1 = ((bf16[64,32,128]{2,1,0:T(8,128)(2,1)}), bf16[64,32,128]{2,1,0:T(8,128)(2,1)S(1)}, u32[]{:S(2)}, u32[]{:S(2)}) async-start(bf16[64,32,128]{2,1,0:T(8,128)(2,1)} %bitcast.24), calls=%async_computation.1 | async-start | bytes 1048576 | tf_op jit(solution)/shard_map/all_to_all | solution.py:183
  111.7 0.8 convolution_bitcast_fusion
  112.8 2.1 %collective-permute-start.8 = (f32[2,64,1024]{2,1,0:T(8,128)S(1)}, f32[2,64,1024]{2,1,0:T(8,128)S(1)}, u32[]{:S(2)}, u32[]{:S(2)}) collective-permute-start(f32[2,64,1024]{2,1,0:T(8,128)S(1)} %fusion.9), channel_id=1, source_target_pairs={{0,1},{1,0},{2,3},{3,2},{4,5},{5,4},{6,7},{7,6},{8,9},{9,8},{10,11... | collective-permute-start | bytes 1572872 | tf_op jit(solution)/shard_map/ppermute | solution.py:21
  114.9 1.8 %collective-permute-done.8 = f32[2,64,1024]{2,1,0:T(8,128)S(1)} collective-permute-done((f32[2,64,1024]{2,1,0:T(8,128)S(1)}, f32[2,64,1024]{2,1,0:T(8,128)S(1)}, u32[]{:S(2)}, u32[]{:S(2)}) %collective-permute-start.8) | collective-permute-done | bytes 524320 | tf_op jit(solution)/shard_map/ppermute | solution.py:21
  116.9 1.2 fusion.13
  118.0 12.3 %all-to-all-done.1 = bf16[64,32,128]{2,1,0:T(8,128)(2,1)S(1)} async-done(((bf16[64,32,128]{2,1,0:T(8,128)(2,1)}), bf16[64,32,128]{2,1,0:T(8,128)(2,1)S(1)}, u32[]{:S(2)}, u32[]{:S(2)}) %all-to-all-start.1) | async-done | bytes 524320 | tf_op jit(solution)/shard_map/all_to_all | solution.py:183
  131.2 0.9 copy.52
  (58 shorter events, 7.4 us)
Async XLA Ops:
  0.6 6.9 %copy-start.4 = (s32[64,2]{0,1:T(2,128)S(1)}, s32[64,2]{0,1:T(2,128)}, u32[]{:S(2)}) copy-start(s32[64,2]{0,1:T(2,128)} %param.7) | copy-start | bytes 1540
  3.9 38.0 %copy-start.3 = (bf16[1,2,1024,64]{2,3,1,0:T(8,128)(2,1)S(1)}, bf16[1,2,1024,64]{2,3,1,0:T(8,128)(2,1)}, u32[]{:S(2)}) copy-start(bf16[1,2,1024,64]{2,3,1,0:T(8,128)(2,1)} %param.11) | copy-start | bytes 786436
  5.0 7.4 %collective-permute-start = (bf16[32,16,128]{2,1,0:T(8,128)(2,1)S(1)}, bf16[32,16,128]{2,1,0:T(8,128)(2,1)S(1)}, u32[]{:S(2)}, u32[]{:S(2)}) collective-permute-start(bf16[32,16,128]{2,1,0:T(8,128)(2,1)S(1)} %fusion.16), channel_id=1, source_target_pairs={{0,2},{1,3},{2,0},{3,1},{4,6},{5,7},{6,4},{7,5},{8,10},{9,11},{10,... | collective-permute-start | bytes 393224 | tf_op jit(solution)/shard_map/ppermute | solution.py:21
  13.9 42.5 %all-to-all-start = ((bf16[64,32,128]{2,1,0:T(8,128)(2,1)}), bf16[64,32,128]{2,1,0:T(8,128)(2,1)S(1)}, u32[]{:S(2)}, u32[]{:S(2)}) async-start(bf16[64,32,128]{2,1,0:T(8,128)(2,1)} %copy.45), calls=%async_computation | async-start | bytes 1048576 | tf_op jit(solution)/shard_map/all_to_all | solution.py:143
  58.5 11.5 %collective-permute-start.4 = (bf16[1024,128]{1,0:T(8,128)(2,1)S(1)}, bf16[1024,128]{1,0:T(8,128)(2,1)S(1)}, u32[]{:S(2)}, u32[]{:S(2)}) collective-permute-start(bf16[1024,128]{1,0:T(8,128)(2,1)S(1)} %bitcast.95), channel_id=1, source_target_pairs={{0,2},{1,3},{2,4},{3,5},{4,6},{5,7},{6,8},{7,9},{8,10},{9,11},{10,... | collective-permute-start | bytes 786440 | tf_op jit(solution)/shard_map/ppermute | solution.py:26
  61.0 10.9 %collective-permute-start.1 = (bf16[1024,128]{1,0:T(8,128)(2,1)S(1)}, bf16[1024,128]{1,0:T(8,128)(2,1)S(1)}, u32[]{:S(2)}, u32[]{:S(2)}) collective-permute-start(bf16[1024,128]{1,0:T(8,128)(2,1)S(1)} %bitcast.96), channel_id=1, source_target_pairs={{0,14},{1,15},{2,0},{3,1},{4,2},{5,3},{6,4},{7,5},{8,6},{9,7},{10,... | collective-permute-start | bytes 786440 | tf_op jit(solution)/shard_map/ppermute | solution.py:26
  70.0 10.6 %collective-permute-start.5 = (bf16[1024,128]{1,0:T(8,128)(2,1)S(1)}, bf16[1024,128]{1,0:T(8,128)(2,1)S(1)}, u32[]{:S(2)}, u32[]{:S(2)}) collective-permute-start(bf16[1024,128]{1,0:T(8,128)(2,1)S(1)} %collective-permute-done.4), channel_id=1, source_target_pairs={{0,2},{1,3},{2,4},{3,5},{4,6},{5,7},{6,8},{7,9},{8,10},{9,11},{10,... | collective-permute-start | bytes 786440 | tf_op jit(solution)/shard_map/ppermute | solution.py:26
  71.9 10.6 %collective-permute-start.2 = (bf16[1024,128]{1,0:T(8,128)(2,1)S(1)}, bf16[1024,128]{1,0:T(8,128)(2,1)S(1)}, u32[]{:S(2)}, u32[]{:S(2)}) collective-permute-start(bf16[1024,128]{1,0:T(8,128)(2,1)S(1)} %collective-permute-done.1), channel_id=1, source_target_pairs={{0,14},{1,15},{2,0},{3,1},{4,2},{5,3},{6,4},{7,5},{8,6},{9,7},{10,... | collective-permute-start | bytes 786440 | tf_op jit(solution)/shard_map/ppermute | solution.py:26
  80.6 9.7 %collective-permute-start.6 = (bf16[1024,128]{1,0:T(8,128)(2,1)S(1)}, bf16[1024,128]{1,0:T(8,128)(2,1)S(1)}, u32[]{:S(2)}, u32[]{:S(2)}) collective-permute-start(bf16[1024,128]{1,0:T(8,128)(2,1)S(1)} %collective-permute-done.5), channel_id=1, source_target_pairs={{0,2},{1,3},{2,4},{3,5},{4,6},{5,7},{6,8},{7,9},{8,10},{9,11},{10,... | collective-permute-start | bytes 786440 | tf_op jit(solution)/shard_map/ppermute | solution.py:26
  82.5 10.0 %collective-permute-start.3 = (bf16[1024,128]{1,0:T(8,128)(2,1)S(1)}, bf16[1024,128]{1,0:T(8,128)(2,1)S(1)}, u32[]{:S(2)}, u32[]{:S(2)}) collective-permute-start(bf16[1024,128]{1,0:T(8,128)(2,1)S(1)} %collective-permute-done.2), channel_id=1, source_target_pairs={{0,14},{1,15},{2,0},{3,1},{4,2},{5,3},{6,4},{7,5},{8,6},{9,7},{10,... | collective-permute-start | bytes 786440 | tf_op jit(solution)/shard_map/ppermute | solution.py:26
  87.9 11.8 %copy-start = (bf16[1,2,1024,1024]{3,2,1,0:T(8,128)(2,1)S(1)}, bf16[1,2,1024,1024]{3,2,1,0:T(8,128)(2,1)}, u32[]{:S(2)}) copy-start(bf16[1,2,1024,1024]{3,2,1,0:T(8,128)(2,1)} %left_ref.1) | copy-start | bytes 12582916
  90.3 9.5 %collective-permute-start.7 = (bf16[1024,128]{1,0:T(8,128)(2,1)S(1)}, bf16[1024,128]{1,0:T(8,128)(2,1)S(1)}, u32[]{:S(2)}, u32[]{:S(2)}) collective-permute-start(bf16[1024,128]{1,0:T(8,128)(2,1)S(1)} %collective-permute-done.6), channel_id=1, source_target_pairs={{0,2},{1,3},{2,4},{3,5},{4,6},{5,7},{6,8},{7,9},{8,10},{9,11},{10,... | collective-permute-start | bytes 786440 | tf_op jit(solution)/shard_map/ppermute | solution.py:26
  105.4 24.9 %all-to-all-start.1 = ((bf16[64,32,128]{2,1,0:T(8,128)(2,1)}), bf16[64,32,128]{2,1,0:T(8,128)(2,1)S(1)}, u32[]{:S(2)}, u32[]{:S(2)}) async-start(bf16[64,32,128]{2,1,0:T(8,128)(2,1)} %bitcast.24), calls=%async_computation.1 | async-start | bytes 1048576 | tf_op jit(solution)/shard_map/all_to_all | solution.py:183
  112.7 4.1 %copy-start.1 = (f32[1,2,64,1024]{3,2,1,0:T(8,128)S(1)}, f32[1,2,64,1024]{3,2,1,0:T(8,128)}, u32[]{:S(2)}) copy-start(f32[1,2,64,1024]{3,2,1,0:T(8,128)} %param.9) | copy-start | bytes 1572868
  112.7 4.1 %copy-start.2 = (f32[1,2,64,1024]{3,2,1,0:T(8,128)S(1)}, f32[1,2,64,1024]{3,2,1,0:T(8,128)}, u32[]{:S(2)}) copy-start(f32[1,2,64,1024]{3,2,1,0:T(8,128)} %param.8) | copy-start | bytes 1572868
  112.8 3.9 %collective-permute-start.8 = (f32[2,64,1024]{2,1,0:T(8,128)S(1)}, f32[2,64,1024]{2,1,0:T(8,128)S(1)}, u32[]{:S(2)}, u32[]{:S(2)}) collective-permute-start(f32[2,64,1024]{2,1,0:T(8,128)S(1)} %fusion.9), channel_id=1, source_target_pairs={{0,1},{1,0},{2,3},{3,2},{4,5},{5,4},{6,7},{7,6},{8,9},{9,8},{10,11... | collective-permute-start | bytes 1572872 | tf_op jit(solution)/shard_map/ppermute | solution.py:21
where the time goes:
time: 133 us; the launch traced here: 132 us
  starting transfers between devices  56.1 us (42%)
  waiting for transfers between devices  45.1 us (34%)
  blocking collectives  8.15 us (6%)
  local copies, waits for them, and re-layouts  7.08 us (5%)
  between operations  4.75 us (4%)
  other arithmetic  4.22 us (3%)
  matrix products  3.65 us (3%)
  Pallas kernels  3.05 us (2%)
    all_to_all x1, starting transfers between devices, local(): lax.all_to_all(outgoing, 'fsdp', split_axis=0, concat_axis=0, tiled=True)  23.4 us
    ppermute x7, starting transfers between devices, passed(): lax.ppermute(value, 'rep', [(r, (r + step) % size) for r in range(size)])  23 us
    ppermute x7, waiting for transfers between devices, passed(): lax.ppermute(value, 'rep', [(r, (r + step) % size) for r in range(size)])  14.8 us
    all_to_all x1, waiting for transfers between devices, local(): lax.all_to_all(returning, 'fsdp', split_axis=0, concat_axis=0, tiled=True)  12.3 us
    all_to_all x1, waiting for transfers between devices, local(): lax.all_to_all(outgoing, 'fsdp', split_axis=0, concat_axis=0, tiled=True)  11.4 us
    all_gather x4, blocking collectives, over_core(): lax.all_gather(value, 'rep', axis_index_groups=[[r, r + 1] for r in range...  8.15 us
    ppermute x2, waiting for transfers between devices, exchanged(): return lax.ppermute(value, 'rep', [(r, r ^ mask) for r in range(size)])  6.49 us
    all_to_all x1, starting transfers between devices, local(): lax.all_to_all(returning, 'fsdp', split_axis=0, concat_axis=0, tiled=True)  5.09 us
  transfers between devices with their start and end apart: 11, of which 8 were waited for; matrix products, arithmetic and copies ran while one was open for 7% of the time, Pallas kernels for 0%

commit v1 on v0

--- a/solution.py
+++ b/solution.py
@@ -159,7 +159,9 @@
     for _ in range(chips // 2 - 1):
         up.append(passed(up[-1], 2))
         down.append(passed(down[-1], -2))
-    far = passed(up[-1], 2)
+    size = lax.axis_size("rep")
+    pairs = [(r, (r + (2 if r % 2 == 0 else -2)) % size) for r in range(size)]
+    far = lax.ppermute(jnp.where(first, up[-1], down[-1]), "rep", pairs)
 
     def part(away, columns):
         rows = taken(right, ((chip + away) % chips).astype(jnp.uint32))

time: 133 us -> 136 us (1.023)
  the two profiles are of different devices: /device:TPU:8 before, /device:TPU:6 now
where the time goes in v1:
time: 136 us; the launch traced here: 135 us
  starting transfers between devices  56.2 us (41%)
  waiting for transfers between devices  48.2 us (35%)
  blocking collectives  8.15 us (6%)
  local copies, waits for them, and re-layouts  7.08 us (5%)
  between operations  4.74 us (3%)
  other arithmetic  4.25 us (3%)
  matrix products  3.68 us (3%)
  Pallas kernels  3.04 us (2%)
    all_to_all x1, starting transfers between devices, local(): lax.all_to_all(outgoing, 'fsdp', split_axis=0, concat_axis=0, tiled=True)  23.1 us
    ppermute x6, starting transfers between devices, passed(): lax.ppermute(value, 'rep', [(r, (r + step) % size) for r in range(size)])  21.5 us
    all_to_all x1, waiting for transfers between devices, local(): lax.all_to_all(returning, 'fsdp', split_axis=0, concat_axis=0, tiled=True)  12.3 us
    ppermute x6, waiting for transfers between devices, passed(): lax.ppermute(value, 'rep', [(r, (r + step) % size) for r in range(size)])  11.9 us
    all_to_all x1, waiting for transfers between devices, local(): lax.all_to_all(outgoing, 'fsdp', split_axis=0, concat_axis=0, tiled=True)  11.4 us
    all_gather x4, blocking collectives, over_core(): lax.all_gather(value, 'rep', axis_index_groups=[[r, r + 1] for r in range...  8.15 us
    ppermute x2, waiting for transfers between devices, exchanged(): return lax.ppermute(value, 'rep', [(r, r ^ mask) for r in range(size)])  6.84 us
    ppermute x1, waiting for transfers between devices, local(): far = lax.ppermute(jnp.where(first, up[-1], down[-1]), 'rep', pairs)  5.73 us
  transfers between devices with their start and end apart: 11, of which 9 were waited for; matrix products, arithmetic and copies ran while one was open for 7% of the time, Pallas kernels for 0%

profile of v1, /device:TPU:6, one launch (start us, length us, event | category | flops | bytes accessed | tf_op | source)
XLA Modules:
  0.0 135.3 jit_solution(18109636354015818883)
XLA Ops:
  0.7 1.0 constant_dynamic-slice_fusion.3
  1.7 2.2 %all_gather.18 = bf16[2,32,16,256]{3,2,1,0:T(8,128)(2,1)S(1)} all-gather(bf16[1,32,16,256]{3,2,1,0:T(8,128)(2,1)S(1)} %constant_dynamic-slice_fusion.3), channel_id=1, replica_groups={{0,1},{2,3},{4,5},{6,7},{8,9},{10,11},{12,13},{14,15},{16,17},{18,19},{..., dimensions={0}, use_global_device_ids=true | all-gather | bytes 786432 | tf_op jit(solution)/shard_map/all_gather | solution.py:13
  3.9 1.1 convert_add_fusion
  5.0 2.4 %collective-permute-start = (bf16[32,16,128]{2,1,0:T(8,128)(2,1)S(1)}, bf16[32,16,128]{2,1,0:T(8,128)(2,1)S(1)}, u32[]{:S(2)}, u32[]{:S(2)}) collective-permute-start(bf16[32,16,128]{2,1,0:T(8,128)(2,1)S(1)} %fusion.16), channel_id=1, source_target_pairs={{0,2},{1,3},{2,0},{3,1},{4,6},{5,7},{6,4},{7,5},{8,10},{9,11},{10,... | collective-permute-start | bytes 393224 | tf_op jit(solution)/shard_map/ppermute | solution.py:21
  7.7 5.0 %collective-permute-done = bf16[32,16,128]{2,1,0:T(8,128)(2,1)S(1)} collective-permute-done((bf16[32,16,128]{2,1,0:T(8,128)(2,1)S(1)}, bf16[32,16,128]{2,1,0:T(8,128)(2,1)S(1)}, u32[]{:S(2)}, u32[]{:S(2)}) %collective-permute-start) | collective-permute-done | bytes 131104 | tf_op jit(solution)/shard_map/ppermute | solution.py:21
  13.0 1.1 copy.45
  14.2 23.1 %all-to-all-start = ((bf16[64,32,128]{2,1,0:T(8,128)(2,1)}), bf16[64,32,128]{2,1,0:T(8,128)(2,1)S(1)}, u32[]{:S(2)}, u32[]{:S(2)}) async-start(bf16[64,32,128]{2,1,0:T(8,128)(2,1)} %copy.45), calls=%async_computation | async-start | bytes 1048576 | tf_op jit(solution)/shard_map/all_to_all | solution.py:143
  41.9 2.0 %all-gather = bf16[2,1,1024,64]{2,3,1,0:T(8,128)(2,1)S(1)} all-gather(bf16[1,1,1024,64]{2,3,1,0:T(8,128)(2,1)S(1)} %constant_dynamic-slice_fusion.1), channel_id=2, replica_groups={{0,1},{2,3},{4,5},{6,7},{8,9},{10,11},{12,13},{14,15},{16,17},{18,19},{..., dimensions={0}, use_global_device_ids=true | all-gather | bytes 393216 | tf_op jit(solution)/shard_map/all_gather | solution.py:13
  44.9 11.4 %all-to-all-done = bf16[64,32,128]{2,1,0:T(8,128)(2,1)S(1)} async-done(((bf16[64,32,128]{2,1,0:T(8,128)(2,1)}), bf16[64,32,128]{2,1,0:T(8,128)(2,1)S(1)}, u32[]{:S(2)}, u32[]{:S(2)}) %all-to-all-start) | async-done | bytes 524320 | tf_op jit(solution)/shard_map/all_to_all | solution.py:143
  56.4 2.0 %all_gather.19 = bf16[2,16,32,128]{3,2,1,0:T(8,128)(2,1)S(1)} all-gather(bf16[1,16,32,128]{3,2,1,0:T(8,128)(2,1)S(1)} %constant_dynamic-slice_fusion), channel_id=1, replica_groups={{0,1},{2,3},{4,5},{6,7},{8,9},{10,11},{12,13},{14,15},{16,17},{18,19},{..., dimensions={0}, use_global_device_ids=true | all-gather | bytes 393216 | tf_op jit(solution)/shard_map/all_gather | solution.py:13
  58.5 4.6 %collective-permute-start.4 = (bf16[1024,128]{1,0:T(8,128)(2,1)S(1)}, bf16[1024,128]{1,0:T(8,128)(2,1)S(1)}, u32[]{:S(2)}, u32[]{:S(2)}) collective-permute-start(bf16[1024,128]{1,0:T(8,128)(2,1)S(1)} %bitcast.95), channel_id=1, source_target_pairs={{0,2},{1,3},{2,4},{3,5},{4,6},{5,7},{6,8},{7,9},{8,10},{9,11},{10,... | collective-permute-start | bytes 786440 | tf_op jit(solution)/shard_map/ppermute | solution.py:26
  63.1 1.9 %collective-permute-start.1 = (bf16[1024,128]{1,0:T(8,128)(2,1)S(1)}, bf16[1024,128]{1,0:T(8,128)(2,1)S(1)}, u32[]{:S(2)}, u32[]{:S(2)}) collective-permute-start(bf16[1024,128]{1,0:T(8,128)(2,1)S(1)} %bitcast.96), channel_id=1, source_target_pairs={{0,14},{1,15},{2,0},{3,1},{4,2},{5,3},{6,4},{7,5},{8,6},{9,7},{10,... | collective-permute-start | bytes 786440 | tf_op jit(solution)/shard_map/ppermute | solution.py:26
  65.7 3.3 %collective-permute-done.4 = bf16[1024,128]{1,0:T(8,128)(2,1)S(1)} collective-permute-done((bf16[1024,128]{1,0:T(8,128)(2,1)S(1)}, bf16[1024,128]{1,0:T(8,128)(2,1)S(1)}, u32[]{:S(2)}, u32[]{:S(2)}) %collective-permute-start.4) | collective-permute-done | bytes 262176 | tf_op jit(solution)/shard_map/ppermute | solution.py:26
  69.0 5.6 %collective-permute-start.5 = (bf16[1024,128]{1,0:T(8,128)(2,1)S(1)}, bf16[1024,128]{1,0:T(8,128)(2,1)S(1)}, u32[]{:S(2)}, u32[]{:S(2)}) collective-permute-start(bf16[1024,128]{1,0:T(8,128)(2,1)S(1)} %collective-permute-done.4), channel_id=1, source_target_pairs={{0,2},{1,3},{2,4},{3,5},{4,6},{5,7},{6,8},{7,9},{8,10},{9,11},{10,... | collective-permute-start | bytes 786440 | tf_op jit(solution)/shard_map/ppermute | solution.py:26
  74.6 1.9 %collective-permute-start.2 = (bf16[1024,128]{1,0:T(8,128)(2,1)S(1)}, bf16[1024,128]{1,0:T(8,128)(2,1)S(1)}, u32[]{:S(2)}, u32[]{:S(2)}) collective-permute-start(bf16[1024,128]{1,0:T(8,128)(2,1)S(1)} %collective-permute-done.1), channel_id=1, source_target_pairs={{0,14},{1,15},{2,0},{3,1},{4,2},{5,3},{6,4},{7,5},{8,6},{9,7},{10,... | collective-permute-start | bytes 786440 | tf_op jit(solution)/shard_map/ppermute | solution.py:26
  77.1 0.9 broadcast_in_dim.27
  78.0 1.6 %collective-permute-done.5 = bf16[1024,128]{1,0:T(8,128)(2,1)S(1)} collective-permute-done((bf16[1024,128]{1,0:T(8,128)(2,1)S(1)}, bf16[1024,128]{1,0:T(8,128)(2,1)S(1)}, u32[]{:S(2)}, u32[]{:S(2)}) %collective-permute-start.5) | collective-permute-done | bytes 262176 | tf_op jit(solution)/shard_map/ppermute | solution.py:26
  79.6 5.6 %collective-permute-start.6 = (bf16[1024,128]{1,0:T(8,128)(2,1)S(1)}, bf16[1024,128]{1,0:T(8,128)(2,1)S(1)}, u32[]{:S(2)}, u32[]{:S(2)}) collective-permute-start(bf16[1024,128]{1,0:T(8,128)(2,1)S(1)} %collective-permute-done.5), channel_id=1, source_target_pairs={{0,2},{1,3},{2,4},{3,5},{4,6},{5,7},{6,8},{7,9},{8,10},{9,11},{10,... | collective-permute-start | bytes 786440 | tf_op jit(solution)/shard_map/ppermute | solution.py:26
  85.2 1.9 %collective-permute-start.3 = (bf16[1024,128]{1,0:T(8,128)(2,1)S(1)}, bf16[1024,128]{1,0:T(8,128)(2,1)S(1)}, u32[]{:S(2)}, u32[]{:S(2)}) collective-permute-start(bf16[1024,128]{1,0:T(8,128)(2,1)S(1)} %collective-permute-done.2), channel_id=1, source_target_pairs={{0,14},{1,15},{2,0},{3,1},{4,2},{5,3},{6,4},{7,5},{8,6},{9,7},{10,... | collective-permute-start | bytes 786440 | tf_op jit(solution)/shard_map/ppermute | solution.py:26
  87.7 1.6 %collective-permute-done.6 = bf16[1024,128]{1,0:T(8,128)(2,1)S(1)} collective-permute-done((bf16[1024,128]{1,0:T(8,128)(2,1)S(1)}, bf16[1024,128]{1,0:T(8,128)(2,1)S(1)}, u32[]{:S(2)}, u32[]{:S(2)}) %collective-permute-start.6) | collective-permute-done | bytes 262176 | tf_op jit(solution)/shard_map/ppermute | solution.py:26
  89.3 5.4 %collective-permute-done.3 = bf16[1024,128]{1,0:T(8,128)(2,1)S(1)} collective-permute-done((bf16[1024,128]{1,0:T(8,128)(2,1)S(1)}, bf16[1024,128]{1,0:T(8,128)(2,1)S(1)}, u32[]{:S(2)}, u32[]{:S(2)}) %collective-permute-start.3) | collective-permute-done | bytes 262176 | tf_op jit(solution)/shard_map/ppermute | solution.py:26
  94.7 1.9 %collective-permute-start.7 = (bf16[1024,128]{1,0:T(8,128)(2,1)S(1)}, bf16[1024,128]{1,0:T(8,128)(2,1)S(1)}, u32[]{:S(2)}, u32[]{:S(2)}) collective-permute-start(bf16[1024,128]{1,0:T(8,128)(2,1)S(1)} %broadcast_select_fusion), channel_id=1, source_target_pairs={{0,2},{1,15},{2,4},{3,1},{4,6},{5,3},{6,8},{7,5},{8,10},{9,7},{10,... | collective-permute-start | bytes 786440 | tf_op jit(solution)/shard_map/ppermute | solution.py:164
  97.2 5.7 %collective-permute-done.7.far_ref = bf16[1024,128]{1,0:T(8,128)(2,1)S(1)} collective-permute-done((bf16[1024,128]{1,0:T(8,128)(2,1)S(1)}, bf16[1024,128]{1,0:T(8,128)(2,1)S(1)}, u32[]{:S(2)}, u32[]{:S(2)}) %collective-permute-start.7) | collective-permute-done | bytes 262176 | tf_op jit(solution)/shard_map/ppermute | solution.py:164
  103.0 3.0 %shard_map.85 = (bf16[4,16,32,128]{3,2,1,0:T(8,128)(2,1)}, bf16[16,32,128]{2,1,0:T(8,128)(2,1)S(1)}) custom-call(s32[1]{0:T(128)} %bitcast.10.core_ref, s32[1]{0:T(128)} %bitcast.11.far_place_ref, s32[1]{0:T(128)} %bitcast.12.own_place_ref, f32[1024,128]{1,0:T(8,128)S(1)} %fusion.2.near_ref, ...), custom_call_target="tpu_custom_call", output_to_operand_aliasing={{0}: (7, {})} | custom-call | tf_op jit(solution)/shard_map/pallas_call | solution.py:75
  106.0 2.0 %all-gather.1 = bf16[32,32,128]{2,1,0:T(8,128)(2,1)S(1)} all-gather(bf16[16,32,128]{2,1,0:T(8,128)(2,1)S(1)} %get-tuple-element.26), channel_id=3, replica_groups={{0,1},{2,3},{4,5},{6,7},{8,9},{10,11},{12,13},{14,15},{16,17},{18,19},{..., dimensions={0}, use_global_device_ids=true | all-gather | bytes 393216 | tf_op jit(solution)/shard_map/all_gather | solution.py:13
  108.7 5.1 %all-to-all-start.1 = ((bf16[64,32,128]{2,1,0:T(8,128)(2,1)}), bf16[64,32,128]{2,1,0:T(8,128)(2,1)S(1)}, u32[]{:S(2)}, u32[]{:S(2)}) async-start(bf16[64,32,128]{2,1,0:T(8,128)(2,1)} %bitcast.24), calls=%async_computation.1 | async-start | bytes 1048576 | tf_op jit(solution)/shard_map/all_to_all | solution.py:185
  115.0 0.8 convolution_bitcast_fusion
  116.0 2.1 %collective-permute-start.8 = (f32[2,64,1024]{2,1,0:T(8,128)S(1)}, f32[2,64,1024]{2,1,0:T(8,128)S(1)}, u32[]{:S(2)}, u32[]{:S(2)}) collective-permute-start(f32[2,64,1024]{2,1,0:T(8,128)S(1)} %fusion.9), channel_id=1, source_target_pairs={{0,1},{1,0},{2,3},{3,2},{4,5},{5,4},{6,7},{7,6},{8,9},{9,8},{10,11... | collective-permute-start | bytes 1572872 | tf_op jit(solution)/shard_map/ppermute | solution.py:21
  118.1 1.8 %collective-permute-done.8 = f32[2,64,1024]{2,1,0:T(8,128)S(1)} collective-permute-done((f32[2,64,1024]{2,1,0:T(8,128)S(1)}, f32[2,64,1024]{2,1,0:T(8,128)S(1)}, u32[]{:S(2)}, u32[]{:S(2)}) %collective-permute-start.8) | collective-permute-done | bytes 524320 | tf_op jit(solution)/shard_map/ppermute | solution.py:21
  120.1 1.2 fusion.13
  121.3 12.3 %all-to-all-done.1 = bf16[64,32,128]{2,1,0:T(8,128)(2,1)S(1)} async-done(((bf16[64,32,128]{2,1,0:T(8,128)(2,1)}), bf16[64,32,128]{2,1,0:T(8,128)(2,1)S(1)}, u32[]{:S(2)}, u32[]{:S(2)}) %all-to-all-start.1) | async-done | bytes 524320 | tf_op jit(solution)/shard_map/all_to_all | solution.py:185
  134.4 0.9 copy.52
  (59 shorter events, 8.1 us)
Async XLA Ops:
  0.6 6.8 %copy-start.4 = (s32[64,2]{0,1:T(2,128)S(1)}, s32[64,2]{0,1:T(2,128)}, u32[]{:S(2)}) copy-start(s32[64,2]{0,1:T(2,128)} %param.7) | copy-start | bytes 1540
  3.9 38.0 %copy-start.3 = (bf16[1,2,1024,64]{2,3,1,0:T(8,128)(2,1)S(1)}, bf16[1,2,1024,64]{2,3,1,0:T(8,128)(2,1)}, u32[]{:S(2)}) copy-start(bf16[1,2,1024,64]{2,3,1,0:T(8,128)(2,1)} %param.11) | copy-start | bytes 786436
  5.0 7.7 %collective-permute-start = (bf16[32,16,128]{2,1,0:T(8,128)(2,1)S(1)}, bf16[32,16,128]{2,1,0:T(8,128)(2,1)S(1)}, u32[]{:S(2)}, u32[]{:S(2)}) collective-permute-start(bf16[32,16,128]{2,1,0:T(8,128)(2,1)S(1)} %fusion.16), channel_id=1, source_target_pairs={{0,2},{1,3},{2,0},{3,1},{4,6},{5,7},{6,4},{7,5},{8,10},{9,11},{10,... | collective-permute-start | bytes 393224 | tf_op jit(solution)/shard_map/ppermute | solution.py:21
  14.2 42.2 %all-to-all-start = ((bf16[64,32,128]{2,1,0:T(8,128)(2,1)}), bf16[64,32,128]{2,1,0:T(8,128)(2,1)S(1)}, u32[]{:S(2)}, u32[]{:S(2)}) async-start(bf16[64,32,128]{2,1,0:T(8,128)(2,1)} %copy.45), calls=%async_computation | async-start | bytes 1048576 | tf_op jit(solution)/shard_map/all_to_all | solution.py:143
  58.5 10.5 %collective-permute-start.4 = (bf16[1024,128]{1,0:T(8,128)(2,1)S(1)}, bf16[1024,128]{1,0:T(8,128)(2,1)S(1)}, u32[]{:S(2)}, u32[]{:S(2)}) collective-permute-start(bf16[1024,128]{1,0:T(8,128)(2,1)S(1)} %bitcast.95), channel_id=1, source_target_pairs={{0,2},{1,3},{2,4},{3,5},{4,6},{5,7},{6,8},{7,9},{8,10},{9,11},{10,... | collective-permute-start | bytes 786440 | tf_op jit(solution)/shard_map/ppermute | solution.py:26
  63.1 11.5 %collective-permute-start.1 = (bf16[1024,128]{1,0:T(8,128)(2,1)S(1)}, bf16[1024,128]{1,0:T(8,128)(2,1)S(1)}, u32[]{:S(2)}, u32[]{:S(2)}) collective-permute-start(bf16[1024,128]{1,0:T(8,128)(2,1)S(1)} %bitcast.96), channel_id=1, source_target_pairs={{0,14},{1,15},{2,0},{3,1},{4,2},{5,3},{6,4},{7,5},{8,6},{9,7},{10,... | collective-permute-start | bytes 786440 | tf_op jit(solution)/shard_map/ppermute | solution.py:26
  69.0 10.6 %collective-permute-start.5 = (bf16[1024,128]{1,0:T(8,128)(2,1)S(1)}, bf16[1024,128]{1,0:T(8,128)(2,1)S(1)}, u32[]{:S(2)}, u32[]{:S(2)}) collective-permute-start(bf16[1024,128]{1,0:T(8,128)(2,1)S(1)} %collective-permute-done.4), channel_id=1, source_target_pairs={{0,2},{1,3},{2,4},{3,5},{4,6},{5,7},{6,8},{7,9},{8,10},{9,11},{10,... | collective-permute-start | bytes 786440 | tf_op jit(solution)/shard_map/ppermute | solution.py:26
  74.6 10.6 %collective-permute-start.2 = (bf16[1024,128]{1,0:T(8,128)(2,1)S(1)}, bf16[1024,128]{1,0:T(8,128)(2,1)S(1)}, u32[]{:S(2)}, u32[]{:S(2)}) collective-permute-start(bf16[1024,128]{1,0:T(8,128)(2,1)S(1)} %collective-permute-done.1), channel_id=1, source_target_pairs={{0,14},{1,15},{2,0},{3,1},{4,2},{5,3},{6,4},{7,5},{8,6},{9,7},{10,... | collective-permute-start | bytes 786440 | tf_op jit(solution)/shard_map/ppermute | solution.py:26
  79.6 9.7 %collective-permute-start.6 = (bf16[1024,128]{1,0:T(8,128)(2,1)S(1)}, bf16[1024,128]{1,0:T(8,128)(2,1)S(1)}, u32[]{:S(2)}, u32[]{:S(2)}) collective-permute-start(bf16[1024,128]{1,0:T(8,128)(2,1)S(1)} %collective-permute-done.5), channel_id=1, source_target_pairs={{0,2},{1,3},{2,4},{3,5},{4,6},{5,7},{6,8},{7,9},{8,10},{9,11},{10,... | collective-permute-start | bytes 786440 | tf_op jit(solution)/shard_map/ppermute | solution.py:26
  85.2 9.5 %collective-permute-start.3 = (bf16[1024,128]{1,0:T(8,128)(2,1)S(1)}, bf16[1024,128]{1,0:T(8,128)(2,1)S(1)}, u32[]{:S(2)}, u32[]{:S(2)}) collective-permute-start(bf16[1024,128]{1,0:T(8,128)(2,1)S(1)} %collective-permute-done.2), channel_id=1, source_target_pairs={{0,14},{1,15},{2,0},{3,1},{4,2},{5,3},{6,4},{7,5},{8,6},{9,7},{10,... | collective-permute-start | bytes 786440 | tf_op jit(solution)/shard_map/ppermute | solution.py:26
  87.7 15.3 %copy-start = (bf16[1,2,1024,1024]{3,2,1,0:T(8,128)(2,1)S(1)}, bf16[1,2,1024,1024]{3,2,1,0:T(8,128)(2,1)}, u32[]{:S(2)}) copy-start(bf16[1,2,1024,1024]{3,2,1,0:T(8,128)(2,1)} %left_ref.1) | copy-start | bytes 12582916
  94.7 8.3 %collective-permute-start.7 = (bf16[1024,128]{1,0:T(8,128)(2,1)S(1)}, bf16[1024,128]{1,0:T(8,128)(2,1)S(1)}, u32[]{:S(2)}, u32[]{:S(2)}) collective-permute-start(bf16[1024,128]{1,0:T(8,128)(2,1)S(1)} %broadcast_select_fusion), channel_id=1, source_target_pairs={{0,2},{1,15},{2,4},{3,1},{4,6},{5,3},{6,8},{7,5},{8,10},{9,7},{10,... | collective-permute-start | bytes 786440 | tf_op jit(solution)/shard_map/ppermute | solution.py:164
  108.7 24.9 %all-to-all-start.1 = ((bf16[64,32,128]{2,1,0:T(8,128)(2,1)}), bf16[64,32,128]{2,1,0:T(8,128)(2,1)S(1)}, u32[]{:S(2)}, u32[]{:S(2)}) async-start(bf16[64,32,128]{2,1,0:T(8,128)(2,1)} %bitcast.24), calls=%async_computation.1 | async-start | bytes 1048576 | tf_op jit(solution)/shard_map/all_to_all | solution.py:185
  115.9 4.1 %copy-start.1 = (f32[1,2,64,1024]{3,2,1,0:T(8,128)S(1)}, f32[1,2,64,1024]{3,2,1,0:T(8,128)}, u32[]{:S(2)}) copy-start(f32[1,2,64,1024]{3,2,1,0:T(8,128)} %param.9) | copy-start | bytes 1572868
  115.9 4.1 %copy-start.2 = (f32[1,2,64,1024]{3,2,1,0:T(8,128)S(1)}, f32[1,2,64,1024]{3,2,1,0:T(8,128)}, u32[]{:S(2)}) copy-start(f32[1,2,64,1024]{3,2,1,0:T(8,128)} %param.8) | copy-start | bytes 1572868
  116.0 3.9 %collective-permute-start.8 = (f32[2,64,1024]{2,1,0:T(8,128)S(1)}, f32[2,64,1024]{2,1,0:T(8,128)S(1)}, u32[]{:S(2)}, u32[]{:S(2)}) collective-permute-start(f32[2,64,1024]{2,1,0:T(8,128)S(1)} %fusion.9), channel_id=1, source_target_pairs={{0,1},{1,0},{2,3},{3,2},{4,5},{5,4},{6,7},{7,6},{8,9},{9,8},{10,11... | collective-permute-start | bytes 1572872 | tf_op jit(solution)/shard_map/ppermute | solution.py:21
